TPU v7x, 32 devices: a whole 2x2x4 slice. The times are simulated.
32 devices in a mesh: sensor: 2 (over core), tm: 16 (over z, y, x).
Axes of the slice: x: 2, y: 2, z: 4, core: 2. Of those that a mesh axis runs over, the one named last changes fastest.
Arguments:
- readings: float32 [512, 128], P(('sensor', 'tm')), may hold values from -18 to 18
- noise_var: float32 [512, 128], P(('sensor', 'tm')), may hold values from 0.1 to 1
- sensor_weights: float32 [512, 64, 128], P(('sensor', 'tm')), may hold values from -0.1 to 1, as said below
- time_weights: float32 [512, 256, 128], P(('sensor', 'tm')), may hold values from -0.1 to 1, as said below
- window_index: int32 [512], P(('sensor', 'tm')), may hold values from 0 to 31
- sensor_kernel: float32 [4096, 4096], P('sensor'), may hold values from -1 to 1.5, as said below
- time_kernel: float32 [4096, 4096], P('tm'), may hold values from -1 to 1.5, as said below
Outputs:
- solution: float32 [512, 128], P(('sensor', 'tm'))
- residual: float32 [512, 128], P(('sensor', 'tm'))
Inputs may be any that keep to these rules, and one draw needn't show every extreme that they name: Block b's readings interpolate from sensor rows 64 * window_index[b] to 64 * window_index[b] + 63 of the sensor rows that its device holds. `sensor_weights`: each reading's column holds the four cubic convolution weights of one position, in rows p - 1 to p + 2 for some p with 1 <= p <= 61; the other entries are zero. `time_weights`: each reading's column holds the four cubic convolution weights of one position, in rows p - 1 to p + 2 for some p with 1 <= p <= 253; the other entries are zero. `sensor_kernel`: symmetric and positive definite. `time_kernel`: symmetric and positive definite.
All inputs are finite; a program needn't handle non-finite values.
Results may differ from a plain program's by a relative error of at most 0.0003.
Values sent between devices are 32-bit elements; how exact they have to be, the bound alone decides.
A program may use at most 192 MiB of HBM per device.

v0:
```python
import jax
import jax.numpy as jnp
from jax import lax
from jax.sharding import PartitionSpec as P

ITERS = 2


PRECISE = lax.Precision.HIGHEST


def on_device(
    readings, noise_var, sensor_weights, time_weights, window_index, sensor_kernel, time_kernel
):
    sensor_dev = sensor_kernel.shape[0]
    time_dev = time_kernel.shape[0]
    win_rows = sensor_weights.shape[1]
    win_count = sensor_dev // win_rows
    window_ids = jnp.arange(win_count, dtype=jnp.int32)
    onehot = (window_index[:, None] == window_ids[None, :]).astype(jnp.float32)
    own_square = lax.dynamic_slice_in_dim(
        sensor_kernel, lax.axis_index("sensor") * sensor_dev, sensor_dev, 1
    )
    own_square = own_square.reshape(win_count, win_rows, win_count, win_rows)
    window_kernel = own_square[window_ids, :, window_ids, :]
    block_kernel = jnp.einsum("bw,wik->bik", onehot, window_kernel, precision=PRECISE)
    sensor_quad = jnp.sum(
        sensor_weights
        * jnp.einsum("bik,bkr->bir", block_kernel, sensor_weights, precision=PRECISE),
        axis=1,
    )
    time_square = lax.dynamic_slice_in_dim(
        time_kernel, lax.axis_index("tm") * time_dev, time_dev, 1
    )
    time_quad = jnp.sum(
        time_weights * jnp.einsum("jl,blr->bjr", time_square, time_weights, precision=PRECISE),
        axis=1,
    )
    inverse = 1.0 / (sensor_quad * time_quad + noise_var)

    def residual_inner(residual, precond):
        return lax.psum(jnp.sum(residual * precond), ("sensor", "tm"))

    residual = readings
    solution = jnp.zeros_like(readings)
    precond = inverse * residual
    direction = precond
    inner_now = residual_inner(residual, precond)
    for iteration in range(ITERS):
        scaled = direction[:, None, :] * time_weights
        contrib = jnp.einsum("bir,bjr->bij", sensor_weights, scaled, precision=PRECISE)
        grid_field = jnp.einsum("bw,bij->wij", onehot, contrib, precision=PRECISE).reshape(
            sensor_dev, time_dev
        )
        left_product = jnp.dot(
            sensor_kernel,
            lax.all_gather(grid_field, "sensor", axis=0, tiled=True),
            precision=PRECISE,
            preferred_element_type=jnp.float32,
        )
        smooth = lax.dot_general(
            lax.all_gather(left_product, "tm", axis=1, tiled=True),
            time_kernel,
            (((1,), (1,)), ((), ())),
            precision=PRECISE,
            preferred_element_type=jnp.float32,
        )
        gathered = jnp.einsum(
            "bw,wij->bij", onehot, smooth.reshape(win_count, win_rows, time_dev), precision=PRECISE
        )
        interp_cols = jnp.einsum("bij,bjr->bir", gathered, time_weights, precision=PRECISE)
        image_vec = jnp.sum(sensor_weights * interp_cols, axis=1) + noise_var * direction
        step_size = inner_now / lax.psum(jnp.sum(direction * image_vec), ("sensor", "tm"))
        solution = solution + step_size * direction
        residual = residual - step_size * image_vec
        if iteration + 1 < ITERS:
            precond = inverse * residual
            inner_next = residual_inner(residual, precond)
            direction = precond + inner_next / inner_now * direction
            inner_now = inner_next
    return (solution, residual)


def solution(mesh):
    in_specs = (
        P(("sensor", "tm"), None),
        P(("sensor", "tm"), None),
        P(("sensor", "tm"), None, None),
        P(("sensor", "tm"), None, None),
        P(("sensor", "tm")),
        P("sensor", None),
        P("tm", None),
    )
    out_specs = (P(("sensor", "tm"), None), P(("sensor", "tm"), None))
    return jax.shard_map(
        on_device, mesh=mesh, in_specs=in_specs, out_specs=out_specs, check_vma=False
    )
```

profile of v0, /device:TPU:0, one launch (start us, length us, event | category | flops | bytes accessed | tf_op | source)
XLA Modules:
  0.0 1206.5 jit_solution(13132646195843724082)
XLA Ops:
  7.2 11.6 constant_dynamic-slice_fusion
  18.8 27.9 %reshape.22 = f32[32,64,32,64]{3,2,1,0:T(8,128)} reshape(f32[2048,2048]{1,0:T(8,128)} %constant_dynamic-slice_fusion) | data formatting | bytes 33554432 | tf_op jit(solution)/shard_map/reshape | solution.py:24
  46.8 31.9 %copy.11 = f32[32,64,32,64]{3,1,2,0:T(8,128)} copy(f32[32,64,32,64]{3,2,1,0:T(8,128)} %reshape.22) | data formatting | bytes 33554432 | tf_op jit(solution)/shard_map/reshape | solution.py:24
  78.7 3.0 gather_fusion
  81.7 2.3 fusion.24
  84.0 0.8 fusion.17
  84.8 3.0 fusion
  87.8 2.4 fusion.9
  90.2 1.6 fusion.22
  91.8 2.5 copy.15
  94.4 16.5 %all-gather.5.cloned.1.call-done = f32[4096,256]{1,0:T(8,128)} async-done(((f32[2048,256]{1,0:T(8,128)}), f32[4096,256]{1,0:T(8,128)}) %all-gather.5.cloned.1.call-update) | async-done | bytes 4194320 | tf_op jit(solution)/shard_map/all_gather | solution.py:57
  110.9 58.9 %convolution_bitcast_fusion.1 = f32[2048,256]{0,1:T(8,128)} fusion(f32[4096,256]{1,0:T(8,128)} %all-gather.5.cloned.1.call-done, f32[2048,4096]{1,0:T(8,128)} %param.12), kind=kOutput, calls=%fused_computation.2 | convolution fusion | flops 25769803776 | bytes 39845888 | tf_op jit(solution)/shard_map/dot_general | solution.py:55
  169.9 352.1 %all-gather.7.cloned.1.call-done = f32[2048,4096]{0,1:T(8,128)} async-done(((f32[2048,256]{0,1:T(8,128)}), f32[2048,4096]{0,1:T(8,128)}) %all-gather.7.cloned.1.call-update) | async-done | bytes 33554448 | tf_op jit(solution)/shard_map/all_gather | solution.py:62
  522.0 57.0 %fusion.45 = f32[2048,256]{1,0:T(8,128)S(1)} fusion(f32[2048,4096]{0,1:T(8,128)} %all-gather.7.cloned.1.call-done, f32[256,4096]{1,0:T(8,128)} %param.13), kind=kOutput, calls=%fused_computation.57 | convolution fusion | flops 25769803776 | bytes 39845888 | tf_op jit(solution)/shard_map/dot_general | solution.py:61
  579.1 2.0 fusion.3
  581.1 2.0 fusion.15
  583.1 0.6 multiply_reduce_fusion.2
  583.7 38.6 %all-reduce = (f32[]{:T(128)}, f32[]{:T(128)}) all-reduce(f32[]{:T(128)} %get-tuple-element.3, f32[]{:T(128)} %get-tuple-element.2), channel_id=1, replica_groups=mesh['sensor'=2,'tm'=16] {'sensor','tm'}, use_global_device_ids=true, to_apply=%region_3.0 | all-reduce | flops 2 | bytes 16 | tf_op jit(solution)/shard_map/psum | solution.py:42
  623.7 0.6 multiply_reduce_fusion.1
  624.3 41.2 %psum.30 = f32[]{:T(128)} all-reduce(f32[]{:T(128)} %multiply_reduce_fusion.1), channel_id=1, replica_groups=mesh['sensor'=2,'tm'=16] {'sensor','tm'}, use_global_device_ids=true, to_apply=%region_8.0 | all-reduce | flops 1 | bytes 8 | tf_op jit(solution)/shard_map/psum | solution.py:42
  666.8 2.4 fusion.12
  669.2 1.6 fusion.19
  670.8 2.5 copy.19
  673.4 13.0 %all-gather.9.cloned.1.call-done = f32[4096,256]{1,0:T(8,128)} async-done(((f32[2048,256]{1,0:T(8,128)}), f32[4096,256]{1,0:T(8,128)}) %all-gather.9.cloned.1.call-update) | async-done | bytes 4194320 | tf_op jit(solution)/shard_map/all_gather | solution.py:57
  686.5 58.7 %convolution_bitcast_fusion = f32[2048,256]{0,1:T(8,128)} fusion(f32[4096,256]{1,0:T(8,128)} %all-gather.9.cloned.1.call-done, f32[2048,4096]{1,0:T(8,128)} %param.12), kind=kOutput, calls=%fused_computation.1 | convolution fusion | flops 25769803776 | bytes 39845888 | tf_op jit(solution)/shard_map/dot_general | solution.py:55
  745.2 352.2 %all-gather.11.cloned.1.call-done = f32[2048,4096]{0,1:T(8,128)} async-done(((f32[2048,256]{0,1:T(8,128)}), f32[2048,4096]{0,1:T(8,128)}) %all-gather.11.cloned.1.call-update) | async-done | bytes 33554448 | tf_op jit(solution)/shard_map/all_gather | solution.py:62
  1097.4 56.9 %fusion.46 = f32[2048,256]{1,0:T(8,128)S(1)} fusion(f32[2048,4096]{0,1:T(8,128)} %all-gather.11.cloned.1.call-done, f32[256,4096]{1,0:T(8,128)} %param.13), kind=kOutput, calls=%fused_computation.58 | convolution fusion | flops 25769803776 | bytes 39845888 | tf_op jit(solution)/shard_map/dot_general | solution.py:61
  1154.3 2.0 fusion.1
  1156.4 2.0 fusion.16
  1158.4 0.6 multiply_reduce_fusion
  1159.0 38.6 %psum.31 = f32[]{:T(128)} all-reduce(f32[]{:T(128)} %multiply_reduce_fusion), channel_id=1, replica_groups=mesh['sensor'=2,'tm'=16] {'sensor','tm'}, use_global_device_ids=true, to_apply=%region_11.0 | all-reduce | flops 1 | bytes 8 | tf_op jit(solution)/shard_map/psum | solution.py:73
  1198.9 0.6 multiply_subtract_fusion
  (21 shorter events, 0.3 us)
Async XLA Ops:
  7.2 103.7 %all-gather.5.cloned.1.call-start = ((), (), s32[]{:S(2)}) async-start(), calls=%async_computation | async-start | bytes 6291456 | tf_op jit(solution)/shard_map/all_gather | solution.py:57
  46.8 34.9 %copy-start.4 = (s32[16]{0:T(128)S(1)}, s32[16]{0:T(128)}, u32[]{:S(2)}) copy-start(s32[16]{0:T(128)} %param.11) | copy-start | bytes 196
  78.7 5.3 copy-start.1
  78.7 6.1 copy-start
  84.0 3.8 copy-start.2
  84.0 3.8 copy-start.3
  94.4 427.7 %all-gather.7.cloned.1.call-start = ((), (), s32[]{:S(2)}) async-start(), calls=%async_computation.1 | async-start | bytes 35651584 | tf_op jit(solution)/shard_map/all_gather | solution.py:62
  169.8 516.6 %all-gather.9.cloned.1.call-start = ((), (), s32[]{:S(2)}) async-start(), calls=%async_computation.2 | async-start | bytes 6291456 | tf_op jit(solution)/shard_map/all_gather | solution.py:57
  673.4 424.0 %all-gather.11.cloned.1.call-start = ((), (), s32[]{:S(2)}) async-start(), calls=%async_computation.3 | async-start | bytes 35651584 | tf_op jit(solution)/shard_map/all_gather | solution.py:62
Sparse Core Ops, SparseCore 0:
  94.5 16.3 all-gather.4
  170.0 352.0 all-gather.6
  673.5 12.9 all-gather.8
  745.3 352.0 all-gather.10
where the time goes:
time: 1210 us
  waiting for transfers between devices  734 us (61%)
  matrix products  254 us (21%)
  blocking collectives  118 us (10%)
  local copies, waits for them, and re-layouts  79.6 us (7%)
  between operations  18.4 us (2%)
    all_gather x2, waiting for transfers between devices, on_device(): lax.all_gather(left_product, 'tm', axis=1, tiled=True)  704 us
    dot_general x2, matrix products, on_device(): jnp.dot(sensor_kernel, lax.all_gather(grid_field, 'sensor', axis=0, tiled...  118 us
    dot_general x2, matrix products, on_device(): lax.dot_general(lax.all_gather(left_product, 'tm', axis=1, tiled=True), t...  114 us
    psum x2, blocking collectives, residual_inner(): return lax.psum(jnp.sum(residual * precond), ('sensor', 'tm'))  79.8 us
    reshape x2, local copies, waits for them, and re-layouts, on_device(): own_square = own_square.reshape(win_count, win_rows, win_count, win_rows)  59.8 us
    psum x1, blocking collectives, on_device(): lax.psum(jnp.sum(direction * image_vec), ('sensor', 'tm'))  38.6 us
    all_gather x2, waiting for transfers between devices, on_device(): lax.all_gather(grid_field, 'sensor', axis=0, tiled=True)  29.5 us
  transfers between devices with their start and end apart: 4, of which 4 were waited for; matrix products, arithmetic and copies ran while one was open for 0% of the time, Pallas kernels for 0%

commit v1 on v0

v1 whole, which is shorter than its diff:
```python
import functools

import jax
import jax.numpy as jnp
from jax import lax
from jax.experimental import pallas as pl
from jax.experimental.pallas import tpu as pltpu
from jax.sharding import PartitionSpec as P

PRECISE = lax.Precision.HIGHEST
F32 = jnp.float32
BF16 = jnp.bfloat16
TAPS = 4
FIELDS = 11
AXES = ("sensor", "tm")


def split(x):
    hi = x.astype(BF16)
    return hi, (x - hi.astype(F32)).astype(BF16)


def dense(taps, first, rows):
    place = lax.broadcasted_iota(jnp.int32, (rows, first.shape[-1]), 0) - first
    out = jnp.where(place == TAPS - 1, taps[TAPS - 1], 0.0)
    for k in range(TAPS - 2, -1, -1):
        out = jnp.where(place == k, taps[k], out)
    return out


def compact_body(group, win_ref, sensor_ref, time_ref, pack_ref):
    step = pl.program_id(0)
    for g in range(group):
        row = pl.ds(step * group + g, 1)
        for ref, taps_at, first_at in ((time_ref, 0, 8), (sensor_ref, TAPS, 9)):
            tile = ref[g]
            ids = lax.broadcasted_iota(jnp.int32, tile.shape, 0)
            first = jnp.min(
                jnp.where(tile != 0.0, ids, tile.shape[0]), axis=0, keepdims=True
            )
            place = ids - first
            for k in range(TAPS):
                pack_ref[taps_at + k, row, :] = jnp.sum(
                    jnp.where(place == k, tile, 0.0), axis=0, keepdims=True
                )
            pack_ref[first_at, row, :] = first.astype(F32)
        window = win_ref[step * group + g]
        pack_ref[10, row, :] = jnp.full((1, tile.shape[1]), window, jnp.int32).astype(F32)


def compact(window_index, sensor_weights, time_weights):
    blocks, win_rows, readings = sensor_weights.shape
    time_dev = time_weights.shape[1]
    group = 4
    return pl.pallas_call(
        functools.partial(compact_body, group),
        grid_spec=pltpu.PrefetchScalarGridSpec(
            num_scalar_prefetch=1,
            grid=(blocks // group,),
            in_specs=[
                pl.BlockSpec((group, win_rows, readings), lambda i, w: (i, 0, 0)),
                pl.BlockSpec((group, time_dev, readings), lambda i, w: (i, 0, 0)),
            ],
            out_specs=pl.BlockSpec((FIELDS, blocks, readings), lambda i, w: (0, 0, 0)),
        ),
        out_shape=jax.ShapeDtypeStruct((FIELDS, blocks, readings), F32),
        name="compact",
    )(window_index, sensor_weights, time_weights)


def inverse_body(group, place_ref, *refs):
    squares = refs[:group]
    time_square, sensor_ref, time_ref, noise_ref, inverse_ref = refs[group:]
    step = pl.program_id(0)
    for g in range(group):
        block = step * group + g
        row = pl.ds(block, 1)
        weights = sensor_ref[g]
        odd = (place_ref[block] % 2).astype(F32)
        both = jnp.concatenate([weights * (1.0 - odd), weights * odd], axis=0)
        mixed = jnp.dot(squares[g][...], both, precision=PRECISE, preferred_element_type=F32)
        sensor_quad = jnp.sum(weights * mixed, axis=0, keepdims=True)
        taps = time_ref[g]
        mixed = jnp.dot(time_square[...], taps, precision=PRECISE, preferred_element_type=F32)
        time_quad = jnp.sum(taps * mixed, axis=0, keepdims=True)
        inverse_ref[row, :] = 1.0 / (sensor_quad * time_quad + noise_ref[row, :])


def inverse_of(noise_var, sensor_weights, time_weights, window_index, sensor_kernel, time_kernel):
    blocks, win_rows, readings = sensor_weights.shape
    time_dev = time_weights.shape[1]
    sensor_dev = sensor_kernel.shape[0]
    group = 4
    place = jnp.concatenate(
        [
            window_index,
            lax.axis_index("sensor")[None].astype(jnp.int32),
            lax.axis_index("tm")[None].astype(jnp.int32),
        ]
    )

    def square(g):
        def where(i, p):
            window = p[i * group + g]
            return window, (p[blocks] * sensor_dev + window * win_rows) // (2 * win_rows)

        return pl.BlockSpec((win_rows, 2 * win_rows), where)

    return pl.pallas_call(
        functools.partial(inverse_body, group),
        grid_spec=pltpu.PrefetchScalarGridSpec(
            num_scalar_prefetch=1,
            grid=(blocks // group,),
            in_specs=[square(g) for g in range(group)]
            + [
                pl.BlockSpec((time_dev, time_dev), lambda i, p: (0, p[blocks + 1])),
                pl.BlockSpec((group, win_rows, readings), lambda i, p: (i, 0, 0)),
                pl.BlockSpec((group, time_dev, readings), lambda i, p: (i, 0, 0)),
                pl.BlockSpec((blocks, readings), lambda i, p: (0, 0)),
            ],
            out_specs=pl.BlockSpec((blocks, readings), lambda i, p: (0, 0)),
        ),
        out_shape=jax.ShapeDtypeStruct((blocks, readings), F32),
        cost_estimate=pl.CostEstimate(
            flops=12 * blocks * time_dev * time_dev * readings,
            bytes_accessed=4 * blocks * time_dev * readings * 4,
            transcendentals=0,
        ),
        name="inverse",
    )(place, *([sensor_kernel] * group), time_kernel, sensor_weights, time_weights, noise_var)


def times_body(pack_ref, kernel_ref, mixed_ref):
    time_dev = kernel_ref.shape[0]
    blocks, readings = pack_ref.shape[2:]
    k_hi, k_lo = split(kernel_ref[...])
    for b in range(0, blocks, 2):
        tiles = []
        for c in (b, b + 1):
            row = slice(c, c + 1)
            taps = [pack_ref[0, k, row, :] for k in range(TAPS)]
            tiles.append(dense(taps, pack_ref[0, 8, row, :].astype(jnp.int32), time_dev))
        w_hi, w_lo = split(jnp.concatenate(tiles, axis=1))
        dot = functools.partial(jnp.dot, preferred_element_type=F32)
        hi, lo = split(dot(k_hi, w_hi) + (dot(k_hi, w_lo) + dot(k_lo, w_hi)))
        for n in range(2):
            part = slice(n * readings, (n + 1) * readings)
            mixed_ref[b + n, :, :readings] = hi[:, part]
            mixed_ref[b + n, :, readings:] = lo[:, part]


def mix_times(pack, time_kernel):
    n_tm, _, blocks, readings = pack.shape
    time_dev = time_kernel.shape[0]
    return pl.pallas_call(
        times_body,
        grid=(n_tm,),
        in_specs=[
            pl.BlockSpec((1, FIELDS, blocks, readings), lambda i: (i, 0, 0, 0)),
            pl.BlockSpec((time_dev, time_dev), lambda i: (0, i)),
        ],
        out_specs=pl.BlockSpec((blocks, time_dev, 2 * readings), lambda i: (i, 0, 0)),
        out_shape=jax.ShapeDtypeStruct((n_tm * blocks, time_dev, 2 * readings), BF16),
        compiler_params=pltpu.CompilerParams(vmem_limit_bytes=40 << 20),
        cost_estimate=pl.CostEstimate(
            flops=6 * n_tm * blocks * time_dev * time_dev * readings,
            bytes_accessed=4 * n_tm * blocks * time_dev * readings,
            transcendentals=0,
        ),
        name="mix_times",
    )(pack, time_kernel)


def field_body(win_rows, win_ref, pack_ref, value_ref, mixed_ref, field_ref):
    step = pl.program_id(0)
    blocks, readings = pack_ref.shape[2:]

    @pl.when(step == 0)
    def _():
        field_ref[...] = jnp.zeros_like(field_ref)

    for b in range(blocks):
        row = slice(b, b + 1)
        value = value_ref[0, row, :]
        taps = [pack_ref[0, TAPS + k, row, :] * value for k in range(TAPS)]
        hi, lo = split(dense(taps, pack_ref[0, 9, row, :].astype(jnp.int32), win_rows))
        left = jnp.concatenate(
            [
                jnp.concatenate([hi, hi], axis=1),
                jnp.concatenate([lo, jnp.zeros_like(lo)], axis=1),
            ],
            axis=0,
        )
        out = lax.dot_general(
            left, mixed_ref[b], (((1,), (1,)), ((), ())), preferred_element_type=F32
        )
        start = pl.multiple_of(win_ref[step * blocks + b] * win_rows, win_rows)
        field_ref[pl.ds(start, win_rows), :] += out[:win_rows] + out[win_rows:]


def field_of(windows, pack, values, mixed, sensor_dev, win_rows):
    n_tm, _, blocks, readings = pack.shape
    time_dev = mixed.shape[1]
    return pl.pallas_call(
        functools.partial(field_body, win_rows),
        grid_spec=pltpu.PrefetchScalarGridSpec(
            num_scalar_prefetch=1,
            grid=(n_tm,),
            in_specs=[
                pl.BlockSpec((1, FIELDS, blocks, readings), lambda i, w: (i, 0, 0, 0)),
                pl.BlockSpec((1, blocks, readings), lambda i, w: (i, 0, 0)),
                pl.BlockSpec((blocks, time_dev, 2 * readings), lambda i, w: (i, 0, 0)),
            ],
            out_specs=pl.BlockSpec((sensor_dev, time_dev), lambda i, w: (0, 0)),
        ),
        out_shape=jax.ShapeDtypeStruct((sensor_dev, time_dev), F32),
        compiler_params=pltpu.CompilerParams(vmem_limit_bytes=40 << 20),
        name="field",
    )(windows, pack, values, mixed)


def image_body(group, chunk, win_ref, *refs):
    kernels = refs[:group]
    field_ref, sensor_ref, time_ref, noise_ref, value_ref, image_ref, halves = refs[group:]
    step = pl.program_id(0)
    time_dev = field_ref.shape[1]
    win_rows = sensor_ref.shape[1]
    sensors = field_ref.shape[0]
    dot = functools.partial(jnp.dot, preferred_element_type=F32)

    @pl.when(step == 0)
    def _():
        for k in range(0, sensors, chunk):
            hi, lo = split(field_ref[k : k + chunk, :])
            halves[k : k + chunk, :time_dev] = hi
            halves[k : k + chunk, time_dev:] = lo

    total = jnp.zeros((group * win_rows, 2 * time_dev), F32)
    extra = jnp.zeros((group * win_rows, time_dev), F32)
    for k in range(0, sensors, chunk):
        left = jnp.concatenate([ref[:, k : k + chunk] for ref in kernels], axis=0)
        hi, lo = split(left)
        total = total + dot(hi, halves[k : k + chunk, :])
        extra = extra + dot(lo, halves[k : k + chunk, :time_dev])
    smooth = total[:, :time_dev] + (total[:, time_dev:] + extra)
    for g in range(group):
        row = pl.ds(step * group + g, 1)
        interp = jnp.dot(
            smooth[g * win_rows : (g + 1) * win_rows],
            time_ref[g],
            precision=PRECISE,
            preferred_element_type=F32,
        )
        image_ref[row, :] = (
            jnp.sum(sensor_ref[g] * interp, axis=0, keepdims=True)
            + noise_ref[row, :] * value_ref[row, :]
        )


def image_of(window_index, sensor_kernel, field, sensor_weights, time_weights, noise_var, value):
    blocks, win_rows, readings = sensor_weights.shape
    sensors, time_dev = field.shape
    group = 4
    chunk = 512

    def rows(g):
        return pl.BlockSpec((win_rows, sensors), lambda i, w: (w[i * group + g], 0))

    return pl.pallas_call(
        functools.partial(image_body, group, chunk),
        grid_spec=pltpu.PrefetchScalarGridSpec(
            num_scalar_prefetch=1,
            grid=(blocks // group,),
            in_specs=[rows(g) for g in range(group)]
            + [
                pl.BlockSpec((sensors, time_dev), lambda i, w: (0, 0)),
                pl.BlockSpec((group, win_rows, readings), lambda i, w: (i, 0, 0)),
                pl.BlockSpec((group, time_dev, readings), lambda i, w: (i, 0, 0)),
                pl.BlockSpec((blocks, readings), lambda i, w: (0, 0)),
                pl.BlockSpec((blocks, readings), lambda i, w: (0, 0)),
            ],
            out_specs=pl.BlockSpec((blocks, readings), lambda i, w: (0, 0)),
            scratch_shapes=[pltpu.VMEM((sensors, 2 * time_dev), BF16)],
        ),
        out_shape=jax.ShapeDtypeStruct((blocks, readings), F32),
        compiler_params=pltpu.CompilerParams(vmem_limit_bytes=48 << 20),
        name="image",
    )(
        window_index,
        *([sensor_kernel] * group),
        field,
        sensor_weights,
        time_weights,
        noise_var,
        value,
    )


def on_device(
    n_sensor,
    n_tm,
    readings,
    noise_var,
    sensor_weights,
    time_weights,
    window_index,
    sensor_kernel,
    time_kernel,
):
    sensor_dev = sensor_kernel.shape[0]
    win_rows = sensor_weights.shape[1]
    blocks = readings.shape[0]
    mine = lax.axis_index("sensor")

    def everywhere(x):
        return lax.all_gather(x, AXES, axis=0, tiled=False)

    pack = lax.all_gather(
        compact(window_index, sensor_weights, time_weights), "tm", axis=0, tiled=False
    )
    inverse = inverse_of(
        noise_var, sensor_weights, time_weights, window_index, sensor_kernel, time_kernel
    )
    start = everywhere(jnp.stack([readings, inverse]))
    windows = pack[:, 10, :, 0].astype(jnp.int32).reshape(-1)
    mixed = mix_times(pack, time_kernel)
    residual_all, inverse_all = start[:, 0], start[:, 1]
    direction_all = inverse_all * residual_all
    direction = inverse * readings
    inner = jnp.sum(residual_all * direction_all)

    def operator_apply(values_all, values):
        own = lax.dynamic_slice_in_dim(values_all, mine * n_tm, n_tm, 0)
        field = field_of(windows, pack, own, mixed, sensor_dev, win_rows)
        field = lax.all_gather(field, "sensor", axis=0, tiled=True)
        return image_of(
            window_index, sensor_kernel, field, sensor_weights, time_weights, noise_var, values
        )

    image = operator_apply(direction_all, direction)
    image_all = everywhere(image)
    step_size = inner / jnp.sum(direction_all * image_all)
    solution = step_size * direction
    residual = readings - step_size * image
    residual_all = residual_all - step_size * image_all
    precond_all = inverse_all * residual_all
    inner_next = jnp.sum(residual_all * precond_all)
    ratio = inner_next / inner
    direction = inverse * residual + ratio * direction
    direction_all = precond_all + ratio * direction_all
    inner = inner_next

    image = operator_apply(direction_all, direction)
    curve = jnp.sum(everywhere(jnp.sum(direction * image, axis=0, keepdims=True)))
    step_size = inner / curve
    return solution + step_size * direction, residual - step_size * image


def solution(mesh):
    in_specs = (
        P(("sensor", "tm"), None),
        P(("sensor", "tm"), None),
        P(("sensor", "tm"), None, None),
        P(("sensor", "tm"), None, None),
        P(("sensor", "tm")),
        P("sensor", None),
        P("tm", None),
    )
    out_specs = (P(("sensor", "tm"), None), P(("sensor", "tm"), None))
    return jax.shard_map(
        functools.partial(on_device, mesh.shape["sensor"], mesh.shape["tm"]),
        mesh=mesh,
        in_specs=in_specs,
        out_specs=out_specs,
        check_vma=False,
    )
```

time: 1210 us -> 381 us (0.31)
  waiting for transfers between devices: 734 us -> 19.9 us
  matrix products: 254 us -> 0 us
  Pallas kernels: 0 us -> 114 us
  blocking collectives: 118 us -> 212 us
  local copies, waits for them, and re-layouts: 79.6 us -> 10.4 us
    all_gather x4 -> x3, waiting for transfers between devices: 734 us -> 19.8 us  [the longest x2 19.8 us: operator_apply(): field = lax.all_gather(field, 'sensor', axis=0, tiled=True)]
    dot_general x15 -> x0, matrix products: 254 us -> none  [the longest x2 118 us: on_device(): jnp.dot(sensor_kernel, lax.all_gather(grid_field, 'sensor', axis=0, tiled...]
    all_gather x0 -> x3, blocking collectives: none -> 212 us  [everywhere(): return lax.all_gather(x, AXES, axis=0, tiled=False)]
    psum x3 -> x0, blocking collectives: 118 us -> none  [the longest x2 79.8 us: residual_inner(): return lax.psum(jnp.sum(residual * precond), ('sensor', 'tm'))]
    pallas_call x0 -> x7, Pallas kernels: none -> 114 us  [the longest x2 44.2 us: field_of(): pl.pallas_call(functools.partial(field_body, win_rows), grid_spec=pltpu.P...]
    reshape x2 -> x0, local copies, waits for them, and re-layouts: 59.8 us -> none  [on_device(): own_square = own_square.reshape(win_count, win_rows, win_count, win_rows)]
  transfers between devices with their start and end apart: 4 -> 3, of which waited for: 4 -> 2; matrix products, arithmetic and copies ran while one was open for 0% -> 1% of each run, Pallas kernels for 0% -> 2%
where the time goes in v1:
time: 381 us; the launch traced here: 380 us
  blocking collectives  212 us (56%)
  Pallas kernels  114 us (30%)
  waiting for transfers between devices  19.9 us (5%)
  between operations  17.9 us (5%)
  local copies, waits for them, and re-layouts  10.4 us (3%)
  other arithmetic  6 us (2%)
    all_gather x3, blocking collectives, everywhere(): return lax.all_gather(x, AXES, axis=0, tiled=False)  212 us
    pallas_call x2, Pallas kernels, field_of(): pl.pallas_call(functools.partial(field_body, win_rows), grid_spec=pltpu.P...  44.2 us
    pallas_call x2, Pallas kernels, image_of(): pl.pallas_call(functools.partial(image_body, group, chunk), grid_spec=plt...  30.5 us
    pallas_call x1, Pallas kernels, mix_times(): pl.pallas_call(times_body, grid=(n_tm,), in_specs=[pl.BlockSpec((1, FIELD...  26.4 us
    all_gather x2, waiting for transfers between devices, operator_apply(): field = lax.all_gather(field, 'sensor', axis=0, tiled=True)  19.8 us
    unnamed x28, local copies, waits for them, and re-layouts  10.3 us
    pallas_call x1, Pallas kernels, inverse_of(): pl.pallas_call(functools.partial(inverse_body, group), grid_spec=pltpu.Pr...  8.23 us
  transfers between devices with their start and end apart: 3, of which 2 were waited for; matrix products, arithmetic and copies ran while one was open for 1% of the time, Pallas kernels for 2%

profile of v1, /device:TPU:0, one launch (start us, length us, event | category | flops | bytes accessed | tf_op | source)
XLA Modules:
  0.0 380.5 jit_solution(14232905947489738565)
XLA Ops:
  7.2 4.9 %compact.1 = f32[11,16,128]{2,1,0:T(8,128)} custom-call(s32[16]{0:T(128)} %win_ref.5, f32[16,64,128]{2,1,0:T(8,128)} %refs_5_.5, f32[16,256,128]{2,1,0:T(8,128)} %refs_6_.5), custom_call_target="tpu_custom_call" | custom-call | tf_op jit(solution)/shard_map/compact/pallas_call | solution.py:55
  12.1 0.0 all-gather.9.cloned.1.call-start
  12.2 1.2 pad_add_fusion.place_ref
  13.4 8.2 %inverse.1 = f32[16,128]{1,0:T(8,128)} custom-call(s32[18]{0:T(128)} %pad_add_fusion.place_ref, f32[2048,4096]{1,0:T(8,128)} %refs_3_.5, f32[2048,4096]{1,0:T(8,128)} %refs_3_.5, f32[2048,4096]{1,0:T(8,128)} %refs_3_.5, f32[2048,4096]{1,0:T(8,128)} %refs_3_.5, f32[256,4096]{1,0:T(8,128)} %kernel_ref.1, f32[16,64,128]{2,1,0:T(8,128)} %refs_5_.5, ...), custom_call_target="tpu_custom_call" | custom-call | flops 1610612736 | bytes 8388608 | tf_op jit(solution)/shard_map/inverse/pallas_call | solution.py:109
  21.7 0.7 pad_maximum_fusion
  22.4 73.6 %all-gather = f32[64,16,128]{2,1,0:T(8,128)S(1)} all-gather(f32[2,16,128]{2,1,0:T(8,128)S(1)} %pad_maximum_fusion), channel_id=2, replica_groups=mesh['sensor'=2,'tm'=16] {'sensor','tm'}, dimensions={0}, use_global_device_ids=true | all-gather | bytes 540672 | tf_op jit(solution)/shard_map/all_gather | solution.py:316
  96.0 0.7 copy-done.11
  96.7 1.4 copy-done.4
  98.1 2.2 copy-done.7
  100.3 26.4 %mix_times.1.mixed_ref = bf16[256,256,256]{2,1,0:T(8,128)(2,1)} custom-call(f32[16,11,16,128]{3,2,1,0:T(8,128)S(1)} %bitcast.35, f32[256,4096]{1,0:T(8,128)S(1)} %copy-done.7), custom_call_target="tpu_custom_call" | custom-call | flops 12884901888 | bytes 33554432 | tf_op jit(solution)/shard_map/mix_times/pallas_call | solution.py:155
  126.6 0.3 fusion.2
  127.0 0.1 convert_element_type.8.win_ref
  127.1 1.4 copy-done.5
  128.5 22.2 %field.2 = f32[2048,256]{1,0:T(8,128)S(1)} custom-call(s32[256]{0:T(256)S(1)} %convert_element_type.8.win_ref, f32[16,11,16,128]{3,2,1,0:T(8,128)S(1)} %bitcast.37, f32[16,16,128]{2,1,0:T(8,128)S(1)} %constant_dynamic-slice_fusion.value_ref, bf16[256,256,256]{2,1,0:T(8,128)(2,1)} %mix_times.1.mixed_ref), custom_call_target="tpu_custom_call" | custom-call | tf_op jit(solution)/shard_map/field/pallas_call | solution.py:204
  150.7 1.3 copy-done.3
  152.0 0.0 all-gather.11.cloned.1.call-start
  152.1 9.9 %all-gather.9.cloned.1.call-done.refs_4_ = f32[4096,256]{1,0:T(8,128)} async-done(((f32[2048,256]{1,0:T(8,128)}), f32[4096,256]{1,0:T(8,128)}) %all-gather.9.cloned.1.call-update) | async-done | bytes 4194320 | tf_op jit(solution)/shard_map/all_gather | solution.py:335
  162.0 15.2 %image.2 = f32[16,128]{1,0:T(8,128)S(1)} custom-call(s32[16]{0:T(128)S(1)} %copy-done.9, f32[2048,4096]{1,0:T(8,128)} %refs_3_.5, f32[2048,4096]{1,0:T(8,128)} %refs_3_.5, f32[2048,4096]{1,0:T(8,128)} %refs_3_.5, f32[2048,4096]{1,0:T(8,128)} %refs_3_.5, f32[4096,256]{1,0:T(8,128)} %all-gather.9.cloned.1.call-done.refs_4_, f32[16,64,128]{2,1,0:T(8,128)S(1)} %copy-done.1, ...), custom_call_target="tpu_custom_call" | custom-call | tf_op jit(solution)/shard_map/image/pallas_call | solution.py:269
  177.3 70.2 %all-gather.2 = f32[512,128]{1,0:T(8,128)S(1)} all-gather(f32[16,128]{1,0:T(8,128)S(1)} %image.2), channel_id=4, replica_groups=mesh['sensor'=2,'tm'=16] {'sensor','tm'}, dimensions={0}, use_global_device_ids=true | all-gather | bytes 270336 | tf_op jit(solution)/shard_map/all_gather | solution.py:316
  247.5 0.7 multiply_reduce_fusion.1
  249.5 0.1 fusion
  249.6 0.7 copy-done.10
  250.2 0.7 multiply_reduce_fusion
  252.3 1.0 dynamic-slice_add_fusion.value_ref
  253.3 1.4 copy-done.6
  254.6 22.0 %field.3 = f32[2048,256]{1,0:T(8,128)S(1)} custom-call(s32[256]{0:T(256)S(1)} %convert_element_type.8.win_ref, f32[16,11,16,128]{3,2,1,0:T(8,128)S(1)} %bitcast.38, f32[16,16,128]{2,1,0:T(8,128)S(1)} %dynamic-slice_add_fusion.value_ref, bf16[256,256,256]{2,1,0:T(8,128)(2,1)} %mix_times.1.mixed_ref), custom_call_target="tpu_custom_call" | custom-call | tf_op jit(solution)/shard_map/field/pallas_call | solution.py:204
  276.6 1.3 copy-done.2
  278.0 9.9 %all-gather.11.cloned.1.call-done.refs_4_ = f32[4096,256]{1,0:T(8,128)} async-done(((f32[2048,256]{1,0:T(8,128)}), f32[4096,256]{1,0:T(8,128)}) %all-gather.11.cloned.1.call-update) | async-done | bytes 4194320 | tf_op jit(solution)/shard_map/all_gather | solution.py:335
  287.9 15.2 %image.3 = f32[16,128]{1,0:T(8,128)S(1)} custom-call(s32[16]{0:T(128)S(1)} %copy-done.9, f32[2048,4096]{1,0:T(8,128)} %refs_3_.5, f32[2048,4096]{1,0:T(8,128)} %refs_3_.5, f32[2048,4096]{1,0:T(8,128)} %refs_3_.5, f32[2048,4096]{1,0:T(8,128)} %refs_3_.5, f32[4096,256]{1,0:T(8,128)} %all-gather.11.cloned.1.call-done.refs_4_, f32[16,64,128]{2,1,0:T(8,128)S(1)} %copy-done.1, ...), custom_call_target="tpu_custom_call" | custom-call | tf_op jit(solution)/shard_map/image/pallas_call | solution.py:269
  303.1 68.2 %all-gather.4 = f32[32,1,128]{2,1,0:T(1,128)S(1)} all-gather(f32[1,1,128]{2,1,0:T(1,128)S(1)} %bitcast.47), channel_id=5, replica_groups=mesh['sensor'=2,'tm'=16] {'sensor','tm'}, dimensions={0}, use_global_device_ids=true | all-gather | bytes 16896 | tf_op jit(solution)/shard_map/all_gather | solution.py:316
  371.3 0.6 reduce
  373.3 0.6 multiply_subtract_fusion.1
  (30 shorter events, 0.2 us)
Async XLA Ops:
  7.2 89.5 %all-gather.13.cloned.1.call-start = ((), (), s32[]{:S(2)}) async-start(), calls=%async_computation.2 | async-start | bytes 1531904 | tf_op jit(solution)/shard_map/all_gather | solution.py:318
  12.1 149.9 %all-gather.9.cloned.1.call-start = ((), (), s32[]{:S(2)}) async-start(), calls=%async_computation | async-start | bytes 6291456 | tf_op jit(solution)/shard_map/all_gather | solution.py:335
  13.4 8.2 %copy-start.13 = (f32[16,128]{1,0:T(8,128)S(1)}, f32[16,128]{1,0:T(8,128)}, u32[]{:S(2)}) copy-start(f32[16,128]{1,0:T(8,128)} %param.7) | copy-start | bytes 24580
  96.0 0.7 copy-start.11
  96.7 1.4 copy-start.4
  98.1 2.2 copy-start.7
  127.1 1.4 copy-start.5
  128.4 23.6 %copy-start.12 = (f32[16,128]{1,0:T(8,128)S(1)}, f32[16,128]{1,0:T(8,128)}, u32[]{:S(2)}) copy-start(f32[16,128]{1,0:T(8,128)} %inverse.1) | copy-start | bytes 24580
  128.4 33.6 %copy-start = (f32[16,256,128]{2,1,0:T(8,128)S(1)}, f32[16,256,128]{2,1,0:T(8,128)}, u32[]{:S(2)}) copy-start(f32[16,256,128]{2,1,0:T(8,128)} %refs_6_.5) | copy-start | bytes 6291460
  128.4 33.6 %copy-start.1 = (f32[16,64,128]{2,1,0:T(8,128)S(1)}, f32[16,64,128]{2,1,0:T(8,128)}, u32[]{:S(2)}) copy-start(f32[16,64,128]{2,1,0:T(8,128)} %refs_5_.5) | copy-start | bytes 1572868
  128.4 33.6 %copy-start.8 = (f32[16,128]{1,0:T(8,128)S(1)}, f32[16,128]{1,0:T(8,128)}, u32[]{:S(2)}) copy-start(f32[16,128]{1,0:T(8,128)} %refs_7_.5) | copy-start | bytes 24580
  128.4 33.6 %copy-start.9 = (s32[16]{0:T(128)S(1)}, s32[16]{0:T(128)}, u32[]{:S(2)}) copy-start(s32[16]{0:T(128)} %win_ref.5) | copy-start | bytes 196
  150.7 1.3 copy-start.3
  152.0 135.8 %all-gather.11.cloned.1.call-start = ((), (), s32[]{:S(2)}) async-start(), calls=%async_computation.1 | async-start | bytes 6291456 | tf_op jit(solution)/shard_map/all_gather | solution.py:335
  249.5 0.7 copy-start.10
  253.2 1.4 copy-start.6
  276.6 1.3 copy-start.2
Sparse Core Ops, SparseCore 0:
  12.3 61.5 all-gather.12
  152.2 9.8 all-gather.8
  278.1 9.7 all-gather.10

commit v2 on v1

--- a/solution.py
+++ b/solution.py
@@ -12,7 +12,6 @@
 BF16 = jnp.bfloat16
 TAPS = 4
 FIELDS = 11
-AXES = ("sensor", "tm")
 
 
 def split(x):
@@ -296,6 +295,72 @@
     )
 
 
+def everywhere_body(n_sensor, n_tm, x_ref, out_ref, send_tm, recv_tm, send_sensor, recv_sensor):
+    here, time = lax.axis_index("sensor"), lax.axis_index("tm")
+    mesh_id = pl.DeviceIdType.MESH
+    barrier = pltpu.get_barrier_semaphore()
+    for d in range(1, n_tm):
+        peer = (here, lax.rem(time + d, n_tm))
+        pl.semaphore_signal(barrier, inc=1, device_id=peer, device_id_type=mesh_id)
+    for d in range(1, n_sensor):
+        peer = (lax.rem(here + d, n_sensor), time)
+        pl.semaphore_signal(barrier, inc=1, device_id=peer, device_id_type=mesh_id)
+    pl.semaphore_wait(barrier, n_tm - 1 + n_sensor - 1)
+
+    copies = []
+    for d in range(1, n_tm):
+        copies.append(
+            pltpu.make_async_remote_copy(
+                src_ref=x_ref,
+                dst_ref=out_ref.at[here * n_tm + time],
+                send_sem=send_tm.at[d - 1],
+                recv_sem=recv_tm.at[d - 1],
+                device_id=(here, lax.rem(time + d, n_tm)),
+                device_id_type=mesh_id,
+            )
+        )
+        copies[-1].start()
+    out_ref[here * n_tm + time] = x_ref[...]
+    for copy in copies:
+        copy.wait()
+    row = out_ref.at[pl.ds(here * n_tm, n_tm)]
+    copies = []
+    for d in range(1, n_sensor):
+        copies.append(
+            pltpu.make_async_remote_copy(
+                src_ref=row,
+                dst_ref=row,
+                send_sem=send_sensor.at[d - 1],
+                recv_sem=recv_sensor.at[d - 1],
+                device_id=(lax.rem(here + d, n_sensor), time),
+                device_id_type=mesh_id,
+            )
+        )
+        copies[-1].start()
+    for copy in copies:
+        copy.wait()
+
+
+def gather_everywhere(n_sensor, n_tm, x, collective_id):
+    dma = pltpu.SemaphoreType.DMA
+    return pl.pallas_call(
+        functools.partial(everywhere_body, n_sensor, n_tm),
+        in_specs=[pl.BlockSpec(memory_space=pltpu.VMEM)],
+        out_specs=pl.BlockSpec(memory_space=pltpu.VMEM),
+        out_shape=jax.ShapeDtypeStruct((n_sensor * n_tm,) + x.shape, x.dtype),
+        scratch_shapes=[
+            dma((n_tm - 1,)),
+            dma((n_tm - 1,)),
+            dma((n_sensor - 1,)),
+            dma((n_sensor - 1,)),
+        ],
+        compiler_params=pltpu.CompilerParams(
+            collective_id=collective_id, has_side_effects=True, vmem_limit_bytes=40 << 20
+        ),
+        name="everywhere",
+    )(x)
+
+
 def on_device(
     n_sensor,
     n_tm,
@@ -312,8 +377,8 @@
     blocks = readings.shape[0]
     mine = lax.axis_index("sensor")
 
-    def everywhere(x):
-        return lax.all_gather(x, AXES, axis=0, tiled=False)
+    def everywhere(x, collective_id):
+        return gather_everywhere(n_sensor, n_tm, x, collective_id)
 
     pack = lax.all_gather(
         compact(window_index, sensor_weights, time_weights), "tm", axis=0, tiled=False
@@ -321,10 +386,10 @@
     inverse = inverse_of(
         noise_var, sensor_weights, time_weights, window_index, sensor_kernel, time_kernel
     )
-    start = everywhere(jnp.stack([readings, inverse]))
+    start = everywhere(jnp.concatenate([readings, inverse], axis=0), 1)
     windows = pack[:, 10, :, 0].astype(jnp.int32).reshape(-1)
     mixed = mix_times(pack, time_kernel)
-    residual_all, inverse_all = start[:, 0], start[:, 1]
+    residual_all, inverse_all = start[:, :blocks], start[:, blocks:]
     direction_all = inverse_all * residual_all
     direction = inverse * readings
     inner = jnp.sum(residual_all * direction_all)
@@ -338,7 +403,7 @@
         )
 
     image = operator_apply(direction_all, direction)
-    image_all = everywhere(image)
+    image_all = everywhere(image, 2)
     step_size = inner / jnp.sum(direction_all * image_all)
     solution = step_size * direction
     residual = readings - step_size * image
@@ -351,7 +416,7 @@
     inner = inner_next
 
     image = operator_apply(direction_all, direction)
-    curve = jnp.sum(everywhere(jnp.sum(direction * image, axis=0, keepdims=True)))
+    curve = jnp.sum(everywhere(direction * image, 2))
     step_size = inner / curve
     return solution + step_size * direction, residual - step_size * image
 

time: 381 us -> 247 us (0.65)
  blocking collectives: 212 us -> 0 us
  waiting for transfers between devices: 19.9 us -> 63.9 us
  Pallas kernels: 114 us -> 147 us
    all_gather x3 -> x0, blocking collectives: 212 us -> none  [everywhere(): return lax.all_gather(x, AXES, axis=0, tiled=False)]
    all_gather x1, waiting for transfers between devices: 0.02 us -> 36.4 us  [on_device(): lax.all_gather(compact(window_index, sensor_weights, time_weights), 'tm',...]
    pallas_call x0 -> x3, Pallas kernels: none -> 33.1 us  [gather_everywhere(): pl.pallas_call(functools.partial(everywhere_body, n_sensor, n_tm), in_spe...]
    all_gather x2, waiting for transfers between devices: 19.8 us -> 27.4 us  [operator_apply(): field = lax.all_gather(field, 'sensor', axis=0, tiled=True)]
    unnamed x28 -> x26, local copies, waits for them, and re-layouts: 10.3 us -> 9.63 us
  transfers between devices with their start and end apart: 3 -> 3, of which waited for: 2 -> 3; matrix products, arithmetic and copies ran while one was open for 1% -> 1% of each run, Pallas kernels for 2% -> 9%
where the time goes in v2:
time: 247 us; the launch traced here: 246 us
  Pallas kernels  147 us (60%)
  waiting for transfers between devices  63.9 us (26%)
  between operations  17.9 us (7%)
  local copies, waits for them, and re-layouts  9.72 us (4%)
  other arithmetic  6.69 us (3%)
    pallas_call x2, Pallas kernels, field_of(): pl.pallas_call(functools.partial(field_body, win_rows), grid_spec=pltpu.P...  44.2 us
    all_gather x1, waiting for transfers between devices, on_device(): lax.all_gather(compact(window_index, sensor_weights, time_weights), 'tm',...  36.4 us
    pallas_call x3, Pallas kernels, gather_everywhere(): pl.pallas_call(functools.partial(everywhere_body, n_sensor, n_tm), in_spe...  33.1 us
    pallas_call x2, Pallas kernels, image_of(): pl.pallas_call(functools.partial(image_body, group, chunk), grid_spec=plt...  30.5 us
    all_gather x2, waiting for transfers between devices, operator_apply(): field = lax.all_gather(field, 'sensor', axis=0, tiled=True)  27.4 us
    pallas_call x1, Pallas kernels, mix_times(): pl.pallas_call(times_body, grid=(n_tm,), in_specs=[pl.BlockSpec((1, FIELD...  26.4 us
    unnamed x26, local copies, waits for them, and re-layouts  9.63 us
    pallas_call x1, Pallas kernels, inverse_of(): pl.pallas_call(functools.partial(inverse_body, group), grid_spec=pltpu.Pr...  8.23 us
  transfers between devices with their start and end apart: 3, of which 3 were waited for; matrix products, arithmetic and copies ran while one was open for 1% of the time, Pallas kernels for 9%

profile of v2, /device:TPU:0, one launch (start us, length us, event | category | flops | bytes accessed | tf_op | source)
XLA Modules:
  0.0 245.8 jit_solution(10206420040973877417)
XLA Ops:
  7.2 0.0 all-gather.9.cloned.1.call-start
  7.2 4.9 %compact.1 = f32[11,16,128]{2,1,0:T(8,128)} custom-call(s32[16]{0:T(128)} %win_ref.5, f32[16,64,128]{2,1,0:T(8,128)} %refs_5_.5, f32[16,256,128]{2,1,0:T(8,128)} %refs_6_.5), custom_call_target="tpu_custom_call" | custom-call | tf_op jit(solution)/shard_map/compact/pallas_call | solution.py:54
  12.1 0.0 all-gather.5.cloned.1.call-start
  12.2 1.3 pad_add_fusion.place_ref
  13.5 8.2 %inverse.1 = f32[16,128]{1,0:T(8,128)} custom-call(s32[18]{0:T(128)} %pad_add_fusion.place_ref, f32[2048,4096]{1,0:T(8,128)} %refs_3_.5, f32[2048,4096]{1,0:T(8,128)} %refs_3_.5, f32[2048,4096]{1,0:T(8,128)} %refs_3_.5, f32[2048,4096]{1,0:T(8,128)} %refs_3_.5, f32[256,4096]{1,0:T(8,128)} %kernel_ref.1, f32[16,64,128]{2,1,0:T(8,128)} %refs_5_.5, ...), custom_call_target="tpu_custom_call" | custom-call | flops 1610612736 | bytes 8388608 | tf_op jit(solution)/shard_map/inverse/pallas_call | solution.py:108
  21.7 0.7 pad_maximum_fusion.x_ref
  22.4 13.6 %everywhere.3 = f32[32,32,128]{2,1,0:T(8,128)S(1)} custom-call(f32[32,128]{1,0:T(8,128)S(1)} %pad_maximum_fusion.x_ref), custom_call_target="tpu_custom_call" | custom-call | tf_op jit(solution)/shard_map/everywhere/pallas_call | solution.py:346
  36.1 0.7 copy-done.10
  36.8 36.4 %all-gather.9.cloned.1.call-done = f32[176,16,128]{2,1,0:T(8,128)} async-done(((f32[11,16,128]{2,1,0:T(8,128)}), f32[176,16,128]{2,1,0:T(8,128)}) %all-gather.9.cloned.1.call-update) | async-done | bytes 1441808 | tf_op jit(solution)/shard_map/all_gather | solution.py:383
  73.2 1.4 copy-done.4
  74.6 2.2 copy-done.7
  76.8 26.4 %mix_times.1.mixed_ref = bf16[256,256,256]{2,1,0:T(8,128)(2,1)} custom-call(f32[16,11,16,128]{3,2,1,0:T(8,128)S(1)} %bitcast.3, f32[256,4096]{1,0:T(8,128)S(1)} %copy-done.7), custom_call_target="tpu_custom_call" | custom-call | flops 12884901888 | bytes 33554432 | tf_op jit(solution)/shard_map/mix_times/pallas_call | solution.py:154
  103.1 0.3 fusion
  103.5 0.1 convert_element_type.8.win_ref
  103.6 1.4 copy-done.5
  105.0 22.2 %field.2 = f32[2048,256]{1,0:T(8,128)S(1)} custom-call(s32[256]{0:T(256)S(1)} %convert_element_type.8.win_ref, f32[16,11,16,128]{3,2,1,0:T(8,128)S(1)} %bitcast.5, f32[16,16,128]{2,1,0:T(8,128)S(1)} %constant_dynamic-slice_fusion.value_ref, bf16[256,256,256]{2,1,0:T(8,128)(2,1)} %mix_times.1.mixed_ref), custom_call_target="tpu_custom_call" | custom-call | tf_op jit(solution)/shard_map/field/pallas_call | solution.py:203
  127.2 1.3 copy-done.3
  128.5 0.2 all-gather.7.cloned.1.call-start
  128.8 12.2 %all-gather.5.cloned.1.call-done.refs_4_ = f32[4096,256]{1,0:T(8,128)} async-done(((f32[2048,256]{1,0:T(8,128)}), f32[4096,256]{1,0:T(8,128)}) %all-gather.5.cloned.1.call-update) | async-done | bytes 4194320 | tf_op jit(solution)/shard_map/all_gather | solution.py:400
  141.0 15.2 %image.2.x_ref = f32[16,128]{1,0:T(8,128)S(1)} custom-call(s32[16]{0:T(128)S(1)} %copy-done.9, f32[2048,4096]{1,0:T(8,128)} %refs_3_.5, f32[2048,4096]{1,0:T(8,128)} %refs_3_.5, f32[2048,4096]{1,0:T(8,128)} %refs_3_.5, f32[2048,4096]{1,0:T(8,128)} %refs_3_.5, f32[4096,256]{1,0:T(8,128)} %all-gather.5.cloned.1.call-done.refs_4_, ...), custom_call_target="tpu_custom_call" | custom-call | tf_op jit(solution)/shard_map/image/pallas_call | solution.py:268
  156.3 9.7 %everywhere.4 = f32[32,16,128]{2,1,0:T(8,128)S(1)} custom-call(f32[16,128]{1,0:T(8,128)S(1)} %image.2.x_ref), custom_call_target="tpu_custom_call" | custom-call | tf_op jit(solution)/shard_map/everywhere/pallas_call | solution.py:346
  166.0 0.7 multiply_reduce_fusion.1
  168.0 1.4 multiply_reduce_fusion
  170.8 1.0 dynamic-slice_add_fusion.value_ref
  171.8 1.4 copy-done.6
  173.1 22.0 %field.3 = f32[2048,256]{1,0:T(8,128)S(1)} custom-call(s32[256]{0:T(256)S(1)} %convert_element_type.8.win_ref, f32[16,11,16,128]{3,2,1,0:T(8,128)S(1)} %bitcast.6, f32[16,16,128]{2,1,0:T(8,128)S(1)} %dynamic-slice_add_fusion.value_ref, bf16[256,256,256]{2,1,0:T(8,128)(2,1)} %mix_times.1.mixed_ref), custom_call_target="tpu_custom_call" | custom-call | tf_op jit(solution)/shard_map/field/pallas_call | solution.py:203
  195.1 1.3 copy-done.2
  196.5 15.2 %all-gather.7.cloned.1.call-done.refs_4_ = f32[4096,256]{1,0:T(8,128)} async-done(((f32[2048,256]{1,0:T(8,128)}), f32[4096,256]{1,0:T(8,128)}) %all-gather.7.cloned.1.call-update) | async-done | bytes 4194320 | tf_op jit(solution)/shard_map/all_gather | solution.py:400
  211.7 15.2 %image.3 = f32[16,128]{1,0:T(8,128)S(1)} custom-call(s32[16]{0:T(128)S(1)} %copy-done.9, f32[2048,4096]{1,0:T(8,128)} %refs_3_.5, f32[2048,4096]{1,0:T(8,128)} %refs_3_.5, f32[2048,4096]{1,0:T(8,128)} %refs_3_.5, f32[2048,4096]{1,0:T(8,128)} %refs_3_.5, f32[4096,256]{1,0:T(8,128)} %all-gather.7.cloned.1.call-done.refs_4_, f32[16,64,128]{2,1,0:T(8,128)S(1)} %copy-done.1, ...), custom_call_target="tpu_custom_call" | custom-call | tf_op jit(solution)/shard_map/image/pallas_call | solution.py:268
  226.9 9.7 %everywhere.5 = f32[32,16,128]{2,1,0:T(8,128)S(1)} custom-call(f32[16,128]{1,0:T(8,128)S(1)} %mul.83.x_ref), custom_call_target="tpu_custom_call" | custom-call | tf_op jit(solution)/shard_map/everywhere/pallas_call | solution.py:346
  236.6 0.7 reduce_sum.39
  238.6 0.6 multiply_subtract_fusion.1
  (27 shorter events, 0.1 us)
Async XLA Ops:
  7.2 66.1 %all-gather.9.cloned.1.call-start = ((), (), s32[]{:S(2)}) async-start(), calls=%async_computation.2 | async-start | bytes 1531904 | tf_op jit(solution)/shard_map/all_gather | solution.py:383
  12.1 128.9 %all-gather.5.cloned.1.call-start = ((), (), s32[]{:S(2)}) async-start(), calls=%async_computation | async-start | bytes 6291456 | tf_op jit(solution)/shard_map/all_gather | solution.py:400
  13.5 8.2 %copy-start.12 = (f32[16,128]{1,0:T(8,128)S(1)}, f32[16,128]{1,0:T(8,128)}, u32[]{:S(2)}) copy-start(f32[16,128]{1,0:T(8,128)} %param.7) | copy-start | bytes 24580
  36.1 0.7 copy-start.10
  73.2 1.4 copy-start.4
  74.6 2.2 copy-start.7
  103.6 1.4 copy-start.5
  104.9 23.8 %copy-start.11 = (f32[16,128]{1,0:T(8,128)S(1)}, f32[16,128]{1,0:T(8,128)}, u32[]{:S(2)}) copy-start(f32[16,128]{1,0:T(8,128)} %inverse.1) | copy-start | bytes 24580
  104.9 36.1 %copy-start = (f32[16,256,128]{2,1,0:T(8,128)S(1)}, f32[16,256,128]{2,1,0:T(8,128)}, u32[]{:S(2)}) copy-start(f32[16,256,128]{2,1,0:T(8,128)} %refs_6_.5) | copy-start | bytes 6291460
  104.9 36.1 %copy-start.1 = (f32[16,64,128]{2,1,0:T(8,128)S(1)}, f32[16,64,128]{2,1,0:T(8,128)}, u32[]{:S(2)}) copy-start(f32[16,64,128]{2,1,0:T(8,128)} %refs_5_.5) | copy-start | bytes 1572868
  104.9 36.1 %copy-start.8 = (f32[16,128]{1,0:T(8,128)S(1)}, f32[16,128]{1,0:T(8,128)}, u32[]{:S(2)}) copy-start(f32[16,128]{1,0:T(8,128)} %refs_7_.5) | copy-start | bytes 24580
  104.9 36.1 %copy-start.9 = (s32[16]{0:T(128)S(1)}, s32[16]{0:T(128)}, u32[]{:S(2)}) copy-start(s32[16]{0:T(128)} %win_ref.5) | copy-start | bytes 196
  127.2 1.3 copy-start.3
  128.5 83.1 %all-gather.7.cloned.1.call-start = ((), (), s32[]{:S(2)}) async-start(), calls=%async_computation.1 | async-start | bytes 6291456 | tf_op jit(solution)/shard_map/all_gather | solution.py:400
  171.8 1.4 copy-start.6
  195.1 1.3 copy-start.2
Sparse Core Ops, SparseCore 0:
  12.3 60.9 all-gather.8
  128.7 12.3 all-gather.4
  196.6 15.0 all-gather.6

commit v3 on v2

--- a/solution.py
+++ b/solution.py
@@ -361,6 +361,47 @@
     )(x)
 
 
+def beside_body(n_sensor, x_ref, out_ref, send, recv):
+    here, time = lax.axis_index("sensor"), lax.axis_index("tm")
+    mesh_id = pl.DeviceIdType.MESH
+    peers = [(lax.rem(here + d, n_sensor), time) for d in range(1, n_sensor)]
+    barrier = pltpu.get_barrier_semaphore()
+    for peer in peers:
+        pl.semaphore_signal(barrier, inc=1, device_id=peer, device_id_type=mesh_id)
+    pl.semaphore_wait(barrier, n_sensor - 1)
+    copies = [
+        pltpu.make_async_remote_copy(
+            src_ref=x_ref,
+            dst_ref=out_ref.at[here],
+            send_sem=send.at[d],
+            recv_sem=recv.at[d],
+            device_id=peer,
+            device_id_type=mesh_id,
+        )
+        for d, peer in enumerate(peers)
+    ]
+    for copy in copies:
+        copy.start()
+    out_ref[here] = x_ref[...]
+    for copy in copies:
+        copy.wait()
+
+
+def gather_beside(n_sensor, x):
+    dma = pltpu.SemaphoreType.DMA
+    return pl.pallas_call(
+        functools.partial(beside_body, n_sensor),
+        in_specs=[pl.BlockSpec(memory_space=pltpu.VMEM)],
+        out_specs=pl.BlockSpec(memory_space=pltpu.VMEM),
+        out_shape=jax.ShapeDtypeStruct((n_sensor,) + x.shape, x.dtype),
+        scratch_shapes=[dma((n_sensor - 1,)), dma((n_sensor - 1,))],
+        compiler_params=pltpu.CompilerParams(
+            collective_id=3, has_side_effects=True, vmem_limit_bytes=40 << 20
+        ),
+        name="beside",
+    )(x).reshape(n_sensor * x.shape[0], x.shape[1])
+
+
 def on_device(
     n_sensor,
     n_tm,
@@ -397,7 +438,7 @@
     def operator_apply(values_all, values):
         own = lax.dynamic_slice_in_dim(values_all, mine * n_tm, n_tm, 0)
         field = field_of(windows, pack, own, mixed, sensor_dev, win_rows)
-        field = lax.all_gather(field, "sensor", axis=0, tiled=True)
+        field = gather_beside(n_sensor, field)
         return image_of(
             window_index, sensor_kernel, field, sensor_weights, time_weights, noise_var, values
         )

time: 247 us -> 227 us (0.919)
  waiting for transfers between devices: 63.9 us -> 36.4 us
  Pallas kernels: 147 us -> 154 us
    all_gather x2 -> x0, waiting for transfers between devices: 27.4 us -> none  [operator_apply(): field = lax.all_gather(field, 'sensor', axis=0, tiled=True)]
    pallas_call x0 -> x2, Pallas kernels: none -> 8.42 us  [gather_beside(): pl.pallas_call(functools.partial(beside_body, n_sensor), in_specs=[pl.Blo...]
  transfers between devices with their start and end apart: 3 -> 1, of which waited for: 3 -> 1; matrix products, arithmetic and copies ran while one was open for 1% -> 1% of each run, Pallas kernels for 9% -> 10%
where the time goes in v3:
time: 227 us; the launch traced here: 226 us
  Pallas kernels  154 us (68%)
  waiting for transfers between devices  36.4 us (16%)
  between operations  18.1 us (8%)
  local copies, waits for them, and re-layouts  9.71 us (4%)
  other arithmetic  7.36 us (3%)
    pallas_call x2, Pallas kernels, field_of(): pl.pallas_call(functools.partial(field_body, win_rows), grid_spec=pltpu.P...  44 us
    all_gather x1, waiting for transfers between devices, on_device(): lax.all_gather(compact(window_index, sensor_weights, time_weights), 'tm',...  36.4 us
    pallas_call x3, Pallas kernels, gather_everywhere(): pl.pallas_call(functools.partial(everywhere_body, n_sensor, n_tm), in_spe...  31.7 us
    pallas_call x2, Pallas kernels, image_of(): pl.pallas_call(functools.partial(image_body, group, chunk), grid_spec=plt...  30.6 us
    pallas_call x1, Pallas kernels, mix_times(): pl.pallas_call(times_body, grid=(n_tm,), in_specs=[pl.BlockSpec((1, FIELD...  26.4 us
    unnamed x26, local copies, waits for them, and re-layouts  9.62 us
    pallas_call x2, Pallas kernels, gather_beside(): pl.pallas_call(functools.partial(beside_body, n_sensor), in_specs=[pl.Blo...  8.42 us
    pallas_call x1, Pallas kernels, inverse_of(): pl.pallas_call(functools.partial(inverse_body, group), grid_spec=pltpu.Pr...  8.24 us
  transfers between devices with their start and end apart: 1, of which 1 were waited for; matrix products, arithmetic and copies ran while one was open for 1% of the time, Pallas kernels for 10%

profile of v3, /device:TPU:0, one launch (start us, length us, event | category | flops | bytes accessed | tf_op | source)
XLA Modules:
  0.0 225.9 jit_solution(16194130458580463180)
XLA Ops:
  7.2 0.0 all-gather.3.cloned.1.call-start
  7.2 4.9 %compact.1 = f32[11,16,128]{2,1,0:T(8,128)} custom-call(s32[16]{0:T(128)} %win_ref.5, f32[16,64,128]{2,1,0:T(8,128)} %refs_5_.5, f32[16,256,128]{2,1,0:T(8,128)} %refs_6_.5), custom_call_target="tpu_custom_call" | custom-call | tf_op jit(solution)/shard_map/compact/pallas_call | solution.py:54
  12.1 0.0 all-gather.3.cloned.1.call-update
  12.2 1.3 pad_add_fusion.place_ref
  13.4 8.2 %inverse.1 = f32[16,128]{1,0:T(8,128)} custom-call(s32[18]{0:T(128)} %pad_add_fusion.place_ref, f32[2048,4096]{1,0:T(8,128)} %refs_3_.5, f32[2048,4096]{1,0:T(8,128)} %refs_3_.5, f32[2048,4096]{1,0:T(8,128)} %refs_3_.5, f32[2048,4096]{1,0:T(8,128)} %refs_3_.5, f32[256,4096]{1,0:T(8,128)} %kernel_ref.1, f32[16,64,128]{2,1,0:T(8,128)} %refs_5_.5, ...), custom_call_target="tpu_custom_call" | custom-call | flops 1610612736 | bytes 8388608 | tf_op jit(solution)/shard_map/inverse/pallas_call | solution.py:108
  21.7 0.7 mul.69.refs_8_
  22.4 0.7 pad_maximum_fusion.x_ref
  23.1 13.5 %everywhere.3 = f32[32,32,128]{2,1,0:T(8,128)S(1)} custom-call(f32[32,128]{1,0:T(8,128)S(1)} %pad_maximum_fusion.x_ref), custom_call_target="tpu_custom_call" | custom-call | tf_op jit(solution)/shard_map/everywhere/pallas_call | solution.py:346
  36.6 0.7 copy-done.10
  37.3 36.4 %all-gather.3.cloned.1.call-done = f32[176,16,128]{2,1,0:T(8,128)} async-done(((f32[11,16,128]{2,1,0:T(8,128)}), f32[176,16,128]{2,1,0:T(8,128)}) %all-gather.3.cloned.1.call-update) | async-done | bytes 1441808 | tf_op jit(solution)/shard_map/all_gather | solution.py:424
  73.7 1.4 copy-done.4
  75.1 2.2 copy-done.7
  77.3 26.4 %mix_times.1.mixed_ref = bf16[256,256,256]{2,1,0:T(8,128)(2,1)} custom-call(f32[16,11,16,128]{3,2,1,0:T(8,128)S(1)} %bitcast.7, f32[256,4096]{1,0:T(8,128)S(1)} %copy-done.7), custom_call_target="tpu_custom_call" | custom-call | flops 12884901888 | bytes 33554432 | tf_op jit(solution)/shard_map/mix_times/pallas_call | solution.py:154
  103.7 0.3 fusion
  104.0 0.1 convert_element_type.8.win_ref
  104.1 22.0 %field.2.x_ref = f32[2048,256]{1,0:T(8,128)S(1)} custom-call(s32[256]{0:T(256)S(1)} %convert_element_type.8.win_ref, f32[16,11,16,128]{3,2,1,0:T(8,128)S(1)} %bitcast.9, f32[16,16,128]{2,1,0:T(8,128)S(1)} %constant_dynamic-slice_fusion.value_ref, bf16[256,256,256]{2,1,0:T(8,128)(2,1)} %mix_times.1.mixed_ref), custom_call_target="tpu_custom_call" | custom-call | tf_op jit(solution)/shard_map/field/pallas_call | solution.py:203
  126.1 0.0 copy-start.3
  126.1 4.2 %beside.2 = f32[2,2048,256]{2,1,0:T(8,128)S(1)} custom-call(f32[2048,256]{1,0:T(8,128)S(1)} %field.2.x_ref), custom_call_target="tpu_custom_call" | custom-call | tf_op jit(solution)/shard_map/beside/pallas_call | solution.py:392
  130.4 2.0 copy-done.1
  132.4 15.2 %image.2.x_ref = f32[16,128]{1,0:T(8,128)S(1)} custom-call(s32[16]{0:T(128)S(1)} %copy-done.9, f32[2048,4096]{1,0:T(8,128)} %refs_3_.5, f32[2048,4096]{1,0:T(8,128)} %refs_3_.5, f32[2048,4096]{1,0:T(8,128)} %refs_3_.5, f32[2048,4096]{1,0:T(8,128)} %refs_3_.5, f32[4096,256]{1,0:T(8,128)} %bitcast.5, f32[16,64,128]{2,1,0:T(8,128)S(1)} %copy-done.3, ...), custom_call_target="tpu_custom_call" | custom-call | tf_op jit(solution)/shard_map/image/pallas_call | solution.py:268
  147.7 8.8 %everywhere.4 = f32[32,16,128]{2,1,0:T(8,128)S(1)} custom-call(f32[16,128]{1,0:T(8,128)S(1)} %image.2.x_ref), custom_call_target="tpu_custom_call" | custom-call | tf_op jit(solution)/shard_map/everywhere/pallas_call | solution.py:346
  156.5 0.7 multiply_reduce_fusion.1
  158.5 1.4 multiply_reduce_fusion
  161.1 1.0 dynamic-slice_add_fusion.value_ref
  162.1 1.4 copy-done.6
  163.5 22.0 %field.3.x_ref = f32[2048,256]{1,0:T(8,128)S(1)} custom-call(s32[256]{0:T(256)S(1)} %convert_element_type.8.win_ref, f32[16,11,16,128]{3,2,1,0:T(8,128)S(1)} %bitcast.10, f32[16,16,128]{2,1,0:T(8,128)S(1)} %dynamic-slice_add_fusion.value_ref, bf16[256,256,256]{2,1,0:T(8,128)(2,1)} %mix_times.1.mixed_ref), custom_call_target="tpu_custom_call" | custom-call | tf_op jit(solution)/shard_map/field/pallas_call | solution.py:203
  185.5 4.2 %beside.3 = f32[2,2048,256]{2,1,0:T(8,128)S(1)} custom-call(f32[2048,256]{1,0:T(8,128)S(1)} %field.3.x_ref), custom_call_target="tpu_custom_call" | custom-call | tf_op jit(solution)/shard_map/beside/pallas_call | solution.py:392
  189.7 1.9 copy-done.2
  191.6 15.4 %image.3 = f32[16,128]{1,0:T(8,128)S(1)} custom-call(s32[16]{0:T(128)S(1)} %copy-done.9, f32[2048,4096]{1,0:T(8,128)} %refs_3_.5, f32[2048,4096]{1,0:T(8,128)} %refs_3_.5, f32[2048,4096]{1,0:T(8,128)} %refs_3_.5, f32[2048,4096]{1,0:T(8,128)} %refs_3_.5, f32[4096,256]{1,0:T(8,128)} %bitcast.6, f32[16,64,128]{2,1,0:T(8,128)S(1)} %copy-done.3, ...), custom_call_target="tpu_custom_call" | custom-call | tf_op jit(solution)/shard_map/image/pallas_call | solution.py:268
  207.0 9.4 %everywhere.5 = f32[32,16,128]{2,1,0:T(8,128)S(1)} custom-call(f32[16,128]{1,0:T(8,128)S(1)} %mul.83.x_ref), custom_call_target="tpu_custom_call" | custom-call | tf_op jit(solution)/shard_map/everywhere/pallas_call | solution.py:346
  216.4 0.7 reduce_sum.39
  218.4 0.6 multiply_subtract_fusion.1
  (23 shorter events, 0.1 us)
Async XLA Ops:
  7.2 66.6 %all-gather.3.cloned.1.call-start = ((), (), s32[]{:S(2)}) async-start(), calls=%async_computation | async-start | bytes 1531904 | tf_op jit(solution)/shard_map/all_gather | solution.py:424
  13.4 8.2 %copy-start.12 = (f32[16,128]{1,0:T(8,128)S(1)}, f32[16,128]{1,0:T(8,128)}, u32[]{:S(2)}) copy-start(f32[16,128]{1,0:T(8,128)} %param.7) | copy-start | bytes 24580
  36.6 0.7 copy-start.10
  73.7 1.4 copy-start.4
  75.1 2.2 copy-start.7
  77.3 26.8 %copy-start.5 = (f32[176,16,128]{2,1,0:T(8,128)S(1)}, f32[176,16,128]{2,1,0:T(8,128)}, u32[]{:S(2)}) copy-start(f32[176,16,128]{2,1,0:T(8,128)} %all-gather.3.cloned.1.call-done) | copy-start | bytes 4325380
  126.1 6.3 %copy-start = (f32[16,256,128]{2,1,0:T(8,128)S(1)}, f32[16,256,128]{2,1,0:T(8,128)}, u32[]{:S(2)}) copy-start(f32[16,256,128]{2,1,0:T(8,128)} %refs_6_.5) | copy-start | bytes 6291460
  126.1 6.3 %copy-start.3 = (f32[16,64,128]{2,1,0:T(8,128)S(1)}, f32[16,64,128]{2,1,0:T(8,128)}, u32[]{:S(2)}) copy-start(f32[16,64,128]{2,1,0:T(8,128)} %refs_5_.5) | copy-start | bytes 1572868
  126.1 6.3 %copy-start.8 = (f32[16,128]{1,0:T(8,128)S(1)}, f32[16,128]{1,0:T(8,128)}, u32[]{:S(2)}) copy-start(f32[16,128]{1,0:T(8,128)} %refs_7_.5) | copy-start | bytes 24580
  126.1 6.3 %copy-start.9 = (s32[16]{0:T(128)S(1)}, s32[16]{0:T(128)}, u32[]{:S(2)}) copy-start(s32[16]{0:T(128)} %win_ref.5) | copy-start | bytes 196
  130.4 2.1 copy-start.1
  132.4 28.6 %copy-start.11 = (f32[16,128]{1,0:T(8,128)S(1)}, f32[16,128]{1,0:T(8,128)}, u32[]{:S(2)}) copy-start(f32[16,128]{1,0:T(8,128)} %inverse.1) | copy-start | bytes 24580
  162.1 1.4 copy-start.6
  189.7 1.9 copy-start.2
Sparse Core Ops, SparseCore 0:
  12.3 61.4 all-gather.2
